TPU v7x, 32 devices: a whole 2x2x4 slice. The times are simulated.
32 devices in a mesh: groups: 2 (over x), ctx: 8 (over z, y), tp: 2 (over core).
Axes of the slice: x: 2, y: 2, z: 4, core: 2. Of those that a mesh axis runs over, the one named last changes fastest.
Arguments:
- query: bfloat16 [2048, 16384], P(('groups', 'ctx'), 'tp'), parts along dimension 0, may hold values from -600 to 600
- key_input: bfloat16 [2048, 1024], P(('groups', 'ctx'), 'tp'), parts along dimension 0, may hold values from -6 to 6
- value: bfloat16 [2048, 1024], P(('groups', 'ctx'), 'tp'), parts along dimension 0, may hold values from -6 to 6
- upstream: bfloat16 [2048, 16384], P(('groups', 'ctx'), 'tp'), parts along dimension 0, may hold values from -0.119628906 to 0.119628906
- output_gradient: bfloat16 [2048, 16384], P(('groups', 'ctx'), 'tp'), parts along dimension 0, may hold values from -0.119628906 to 0.119628906
- down_adapter: bfloat16 [16384, 32], P('tp'), may hold values from -0.046875 to 0.046875
- up_adapter: bfloat16 [32, 16384], P(None, 'tp'), may hold values from -1 to 1
- document_length_list: int32 [64], P('groups'), parts along dimension 0, may hold values from 1 to 64, 1024 in all
Outputs:
- query_gradient_full: bfloat16 [2048, 16384], P(('groups', 'ctx'), 'tp'), parts along dimension 0
- key_gradient_full: bfloat16 [2048, 1024], P(('groups', 'ctx'), 'tp'), parts along dimension 0
- value_gradient_full: bfloat16 [2048, 1024], P(('groups', 'ctx'), 'tp'), parts along dimension 0
- down_adapter_gradient: float32 [32768, 32], P(('groups', 'tp')), parts along dimension 0
- up_adapter_gradient: float32 [64, 16384], P('groups', 'tp'), parts along dimension 0
There are 2 independent parts, one for each index of `groups`. A program takes and returns all parts, laid end to end along the dimension named above; an argument that names none is the same for every part. Nothing has to cross between parts.
Inputs may be any that keep to these rules, and one draw needn't show every extreme that they name: `document_length_list`: lengths of 32 documents that together fill all 1024 positions; the longest is exactly 64.
All inputs are finite; a program needn't handle non-finite values.
Results may differ from a plain program's by a relative error of at most 0.012.
The roundings to bfloat16 on the way count: a program that leaves them out, or rounds other values in their place, can miss the bound.
Values may be sent and summed in bfloat16 or wider, within the bound.
A program may use at most 128 MiB of HBM per device.

v0:
```python
import jax
import jax.numpy as jnp
from jax import lax
from jax.sharding import PartitionSpec as P

HEAD_SIZE = 128


NEG = -1e30
ADAPTER_SCALE = 0.5


def passed_along(block, axis, distance):
    devices = range(lax.axis_size(axis))
    route = [(i - distance, i) for i in devices if i - distance in devices]
    return lax.ppermute(block, axis, route)


def token_layout(device, row_count, ctx_size, starts):
    half_rows = row_count // 2
    offset = jnp.arange(row_count, dtype=jnp.int32)
    stretch_index = jnp.where(offset < half_rows, device, 2 * ctx_size - 1 - device)
    token_position = stretch_index * half_rows + offset % half_rows
    inside = jnp.logical_and(device >= 0, device < ctx_size)
    doc_owner = jnp.sum((starts[None, :] <= token_position[:, None]).astype(jnp.int32), axis=1) - 1
    return (token_position, jnp.where(inside, doc_owner, -2))


def block_scores(queries, keys_here, allowed, score_scale):
    scores = (
        jnp.einsum("qkgd,skd->kgqs", queries, keys_here, preferred_element_type=jnp.float32)
        * score_scale
    )
    return jnp.where(allowed[None, None], scores, NEG)


def block_forward(scores, row_top, row_total, values_here):
    prob_full = jnp.exp(scores - row_top[..., None]) / row_total[..., None]
    prob_low = prob_full.astype(jnp.bfloat16)
    partial_out = jnp.einsum(
        "kgqs,skd->qkgd", prob_low, values_here, preferred_element_type=jnp.float32
    )
    return (prob_full, prob_low, partial_out)


def block_backward(
    prob_full, prob_low, row_delta, heads_grad, queries, keys_here, values_here, score_scale
):
    dprobs = jnp.einsum(
        "qkgd,skd->kgqs", heads_grad, values_here, preferred_element_type=jnp.float32
    )
    dscores = (prob_full * (dprobs - row_delta[..., None])).astype(jnp.bfloat16)
    part_query = jnp.einsum(
        "kgqs,skd->qkgd", dscores, keys_here, preferred_element_type=jnp.float32
    )
    part_key = score_scale * jnp.einsum(
        "kgqs,qkgd->skd", dscores, queries, preferred_element_type=jnp.float32
    )
    part_value = jnp.einsum(
        "kgqs,qkgd->skd", prob_low, heads_grad, preferred_element_type=jnp.float32
    )
    return (part_query, part_key, part_value)


def shards(
    query,
    key_input,
    value,
    upstream,
    output_gradient,
    down_adapter,
    up_adapter,
    document_length_list,
):
    row_count = query.shape[0]
    half_rows = row_count // 2
    kv_width = key_input.shape[1]
    kv_heads = kv_width // HEAD_SIZE
    query_group_size = query.shape[1] // kv_width
    ctx_size = lax.axis_size("ctx")
    ctx_index = lax.axis_index("ctx")
    score_scale = HEAD_SIZE ** (-0.5)
    starts = jnp.cumsum(document_length_list) - document_length_list
    own_pos, own_doc = token_layout(ctx_index, row_count, ctx_size, starts)
    queries = query.reshape(row_count, kv_heads, query_group_size, HEAD_SIZE)
    inner_portion = jnp.dot(output_gradient, up_adapter.T, preferred_element_type=jnp.float32)
    inner_sum = lax.psum(inner_portion, "tp")
    packed = jnp.concatenate([key_input, value], axis=1)
    lower_rows = passed_along(packed[:half_rows], "ctx", 1)
    upper_rows = passed_along(packed[half_rows:], "ctx", -1)
    kv_blocks = [lower_rows, packed, upper_rows]
    key_ranges = [(0, half_rows), (0, row_count), (half_rows, row_count)]
    strides = (-1, 0, 1)
    keys_list = []
    values_list = []
    scores_list = []
    guard_list = []
    for stride, kv_block, key_range in zip(strides, kv_blocks, key_ranges):
        key_count = kv_block.shape[0]
        keys_here = kv_block[:, :kv_width].reshape(key_count, kv_heads, HEAD_SIZE)
        values_here = kv_block[:, kv_width:].reshape(key_count, kv_heads, HEAD_SIZE)
        key_pos, key_doc = token_layout(ctx_index + stride, row_count, ctx_size, starts)
        key_pos = key_pos[key_range[0] : key_range[1]]
        key_doc = key_doc[key_range[0] : key_range[1]]
        allowed = jnp.logical_and(
            own_doc[:, None] == key_doc[None, :], key_pos[None, :] <= own_pos[:, None]
        )
        active = jnp.any(allowed)
        scores = block_scores(queries, keys_here, allowed, score_scale)
        keys_list.append(keys_here)
        values_list.append(values_here)
        scores_list.append(scores)
        guard_list.append((False, active))
    row_top = jnp.max(scores_list[0], axis=-1)
    for scores in scores_list[1:]:
        row_top = jnp.maximum(row_top, jnp.max(scores, axis=-1))
    row_total = jnp.zeros_like(row_top)
    for scores in scores_list:
        row_total = row_total + jnp.sum(jnp.exp(scores - row_top[..., None]), axis=-1)
    head_shape = (row_count, kv_heads, query_group_size, HEAD_SIZE)
    forward_list = []
    out_total = jnp.zeros(head_shape, jnp.float32)
    for scores, values_here, guard in zip(scores_list, values_list, guard_list):
        result = block_forward(scores, row_top, row_total, values_here)
        forward_list.append(result)
        out_total = out_total + result[2]
    attn_out = lax.optimization_barrier(out_total.astype(jnp.bfloat16))
    attention_flat = attn_out.reshape(row_count, kv_heads * query_group_size * HEAD_SIZE)
    outer_portion = jnp.dot(attention_flat, down_adapter, preferred_element_type=jnp.float32)
    outer_sum = lax.psum(outer_portion, "tp")
    inner_lower = inner_sum.astype(jnp.bfloat16)
    outer_lower = outer_sum.astype(jnp.bfloat16)
    attention_gradient = (
        upstream.astype(jnp.float32)
        + ADAPTER_SCALE * jnp.dot(inner_lower, down_adapter.T, preferred_element_type=jnp.float32)
    ).astype(jnp.bfloat16)
    heads_grad = attention_gradient.reshape(head_shape)
    row_delta = jnp.sum(
        heads_grad.astype(jnp.float32) * attn_out.astype(jnp.float32), axis=-1
    ).transpose(1, 2, 0)
    query_total = jnp.zeros(head_shape, jnp.float32)
    grads_list = []
    for keys_here, values_here, forward_parts, guard in zip(
        keys_list, values_list, forward_list, guard_list
    ):
        kv_shape = keys_here.shape
        result = block_backward(
            forward_parts[0],
            forward_parts[1],
            row_delta,
            heads_grad,
            queries,
            keys_here,
            values_here,
            score_scale,
        )
        query_total = query_total + result[0]
        key_count = kv_shape[0]
        grads_list.append(
            jnp.concatenate(
                [result[1].reshape(key_count, kv_width), result[2].reshape(key_count, kv_width)],
                axis=1,
            )
        )
    kv_total = grads_list[1]
    lower_back = passed_along(grads_list[0].astype(jnp.bfloat16), "ctx", -1).astype(jnp.float32)
    upper_back = passed_along(grads_list[2].astype(jnp.bfloat16), "ctx", 1).astype(jnp.float32)
    kv_total = kv_total + jnp.concatenate([lower_back, upper_back], axis=0)
    query_gradient_full = (
        (score_scale * query_total)
        .reshape(row_count, kv_heads * query_group_size * HEAD_SIZE)
        .astype(jnp.bfloat16)
    )
    key_gradient_full = kv_total[:, :kv_width].astype(jnp.bfloat16)
    value_gradient_full = kv_total[:, kv_width:].astype(jnp.bfloat16)
    down_adapter_gradient = ADAPTER_SCALE * jnp.einsum(
        "tf,tr->fr", attention_flat, inner_lower, preferred_element_type=jnp.float32
    )
    up_adapter_gradient = ADAPTER_SCALE * jnp.einsum(
        "tr,tc->rc", outer_lower, output_gradient, preferred_element_type=jnp.float32
    )
    down_adapter_gradient, up_adapter_gradient = lax.psum(
        (down_adapter_gradient, up_adapter_gradient), "ctx"
    )
    return (
        query_gradient_full,
        key_gradient_full,
        value_gradient_full,
        down_adapter_gradient,
        up_adapter_gradient,
    )


def solution(mesh):
    in_specs = (
        P(("groups", "ctx"), "tp"),
        P(("groups", "ctx"), "tp"),
        P(("groups", "ctx"), "tp"),
        P(("groups", "ctx"), "tp"),
        P(("groups", "ctx"), "tp"),
        P("tp", None),
        P(None, "tp"),
        P("groups"),
    )
    out_specs = (
        P(("groups", "ctx"), "tp"),
        P(("groups", "ctx"), "tp"),
        P(("groups", "ctx"), "tp"),
        P(("groups", "tp"), None),
        P("groups", "tp"),
    )
    return jax.shard_map(shards, mesh=mesh, in_specs=in_specs, out_specs=out_specs, check_vma=False)
```

profile of v0, /device:TPU:0, one launch (start us, length us, event | category | flops | bytes accessed | tf_op | source)
XLA Modules:
  0.0 228.4 jit_solution(13514725805919430899)
XLA Ops:
  10.5 5.5 %collective-permute-start = (bf16[64,1024]{1,0:T(8,128)(2,1)S(1)}, bf16[64,1024]{1,0:T(8,128)(2,1)S(1)}, u32[]{:S(2)}, u32[]{:S(2)}) collective-permute-start(bf16[64,1024]{1,0:T(8,128)(2,1)S(1)} %get-tuple-element.32), channel_id=1, source_target_pairs={{0,2},{2,4},{4,6},{6,8},{8,10},{10,12},{12,14},{1,3},{3,5},{5,7},{... | collective-permute-start | bytes 393224 | tf_op jit(solution)/shard_map/ppermute | solution.py:16
  20.4 3.6 %copy.165 = bf16[16,8,64,128]{3,2,1,0:T(8,128)(2,1)} copy(bf16[16,8,64,128]{3,1,2,0:T(8,128)(2,1)} %bitcast.191) | data formatting | bytes 4194304
  25.9 4.0 %fusion.9 = (f32[4,16,128]{2,1,0:T(8,128)S(1)}, f32[4,128,128,16]{2,1,3,0:T(8,128)}) fusion(pred[128,128]{0,1:T(8,128)(4,1)S(1)} %compare_and_fusion, bf16[128,4,128,1]{0,2,3,1:T(8,128)(2,1)S(1)} %copy.130, bf16[128,4,16,128]{3,2,1,0:T(8,128)(2,1)S(1)} %bitcast.179), kind=kOutput, calls=%fused_computation.20 | convolution fusion | flops 271572992 | bytes 6471680 | tf_op jit(solution)/shard_map/qkgd,skd->kgqs/dot_general | solution.py:31
  30.7 3.4 %fusion.61 = (f32[4,16,128]{2,1,0:T(8,128)S(1)}, f32[4,16,128,64]{2,3,1,0:T(8,128)S(1)}) fusion(bf16[128,4,16,128]{3,2,1,0:T(8,128)(2,1)} %bitcast.178, bf16[64,4,128,1]{2,1,0,3:T(4,128)(2,1)S(1)} %bitcast.192, pred[128,64]{0,1:T(8,128)(4,1)S(1)} %get-tuple-element.39), kind=kOutput, calls=%fused_computation.108 | convolution fusion | flops 135782400 | bytes 4300800 | tf_op jit(solution)/shard_map/qkgd,skd->kgqs/dot_general | solution.py:31
  35.9 1.9 copy-done.1
  41.8 2.5 %fusion.37 = bf16[4,16,128,128]{2,3,1,0:T(8,128)(2,1)} fusion(f32[4,16,128]{2,1,0:T(8,128)S(1)} %add_add_fusion, f32[4,16,128]{2,1,0:T(8,128)S(1)} %maximum_maximum_fusion, f32[4,128,128,16]{2,1,3,0:T(8,128)S(1)} %copy-done.1, pred[128,128]{0,1:T(8,128)(4,1)S(1)} %compare_and_fusion), kind=kLoop, calls=%fused_computation.59 | loop fusion | flops 5242880 | bytes 6373376 | tf_op jit(solution)/shard_map/convert_element_type | solution.py:39
  45.0 3.7 %copy.110 = bf16[4,16,128,64]{3,1,0,2:T(8,128)(2,1)} copy(bf16[4,16,128,64]{2,3,1,0:T(8,128)(2,1)S(1)} %get-tuple-element.38) | data formatting | bytes 2097152 | tf_op jit(solution)/shard_map/convert_element_type | solution.py:39
  48.7 2.7 %fusion.46 = f32[4,128,16,128]{3,1,2,0:T(8,128)} fusion(bf16[4,16,128,64]{2,3,1,0:T(8,128)(2,1)S(1)} %get-tuple-element.38, bf16[64,4,128,1]{2,1,0,3:T(4,128)(2,1)S(1)} %bitcast.208), kind=kOutput, calls=%fused_computation.76 | convolution fusion | flops 134217728 | bytes 5308416 | tf_op jit(solution)/shard_map/kgqs,skd->qkgd/dot_general | solution.py:40
  52.3 4.7 %copy.114 = bf16[4,16,128,64]{3,1,0,2:T(8,128)(2,1)} copy(bf16[4,16,128,64]{2,3,1,0:T(8,128)(2,1)} %get-tuple-element.37) | data formatting | bytes 2097152 | tf_op jit(solution)/shard_map/convert_element_type | solution.py:39
  57.0 2.5 %fusion.42 = f32[4,16,128,128]{2,3,1,0:T(8,128)S(1)} fusion(bf16[4,16,128,128]{2,3,1,0:T(8,128)(2,1)} %fusion.37, bf16[128,4,128,1]{2,1,0,3:T(4,128)(2,1)S(1)} %bitcast.197), kind=kOutput, calls=%fused_computation.67 | convolution fusion | flops 268435456 | bytes 6422528 | tf_op jit(solution)/shard_map/kgqs,skd->qkgd/dot_general | solution.py:40
  62.7 4.0 %all-reduce.1 = (bf16[128,32]{0,1:T(8,128)(2,1)S(1)}, bf16[128,32]{0,1:T(8,128)(2,1)}) all-reduce(f32[128,32]{0,1:T(8,128)S(1)} %copy-done.29, f32[128,32]{0,1:T(8,128)S(1)} %fusion.66), channel_id=1, replica_groups=mesh['groups'=2,'ctx'=8,'tp'=2] {'tp'}, use_global_device_ids=true, to_apply=%region_10.11 | all-reduce | flops 8192 | bytes 49152 | tf_op jit(solution)/shard_map/psum | solution.py:87
  66.7 3.5 %convolution_multiply_fusion.2 = f32[8192,32]{0,1:T(8,128)} fusion(bf16[128,8192]{0,1:T(8,128)(2,1)} %bitcast.189, bf16[128,32]{0,1:T(8,128)(2,1)S(1)} %get-tuple-element.27), kind=kOutput, calls=%fused_computation.4 | convolution fusion | flops 67371008 | bytes 3153920 | tf_op jit(solution)/shard_map/tf,tr->fr/dot_general | solution.py:176
  71.0 1.9 copy.166
  73.0 4.5 %copy.88 = bf16[128,4,16,128]{0,3,2,1:T(8,128)(2,1)} copy(bf16[128,4,16,128]{3,2,1,0:T(8,128)(2,1)} %bitcast.184) | data formatting | bytes 4194304 | tf_op jit(solution)/shard_map/reshape | solution.py:137
  77.5 3.2 %multiply_reduce_fusion = f32[128,4,16]{0,2,1:T(8,128)S(1)} fusion(bf16[128,4,16,128]{0,3,2,1:T(8,128)(2,1)} %copy-done.8, bf16[128,4,16,128]{0,3,2,1:T(8,128)(2,1)} %copy.88), kind=kLoop, calls=%fused_computation.16 | loop fusion | flops 4186112 | bytes 4227072 | tf_op jit(solution)/shard_map/reduce_sum | solution.py:138
  84.5 4.6 %copy.105 = bf16[4,16,128,128]{3,1,0,2:T(8,128)(2,1)} copy(bf16[4,16,128,128]{2,3,1,0:T(8,128)(2,1)} %fusion.37) | data formatting | bytes 4194304 | tf_op jit(solution)/shard_map/convert_element_type | solution.py:39
  89.1 5.7 %fusion.5 = bf16[4,16,128,128]{2,3,1,0:T(8,128)(2,1)} fusion(bf16[128,4,16,128]{0,3,2,1:T(8,128)(2,1)} %copy.88, f32[4,16,128]{2,1,0:T(8,128)S(1)} %bitcast.211, f32[4,16,128]{2,1,0:T(8,128)S(1)} %add_add_fusion, f32[4,16,128]{2,1,0:T(8,128)S(1)} %maximum_maximum_fusion, f32[4,128,128,16]{2,1,3,0:T(8,128)} %get-tuple-element.46, ...), kind=kOutput, calls=%fused_computation.11 | convolution fusion | flops 275775488 | bytes 8634368 | tf_op jit(solution)/shard_map/qkgd,skd->kgqs/dot_general | solution.py:49
  96.2 3.2 %fusion.29 = bf16[4,8,8,128]{3,2,1,0:T(8,128)(2,1)S(1)} fusion(bf16[128,4,16,128]{3,2,1,0:T(8,128)(2,1)} %bitcast.185, bf16[4,16,128,64]{3,1,0,2:T(8,128)(2,1)} %copy.110), kind=kOutput, calls=%fused_computation.51 | convolution fusion | flops 134250496 | bytes 3211264 | tf_op jit(solution)/shard_map/kgqs,qkgd->skd/dot_general | solution.py:59
  105.9 6.1 %collective-permute-start.3 = (bf16[64,1024]{1,0:T(8,128)(2,1)}, bf16[64,1024]{1,0:T(8,128)(2,1)}, u32[]{:S(2)}, u32[]{:S(2)}) collective-permute-start(bf16[64,1024]{1,0:T(8,128)(2,1)} %pad_maximum_fusion.1), channel_id=1, source_target_pairs={{0,2},{2,4},{4,6},{6,8},{8,10},{10,12},{12,14},{1,3},{3,5},{5,7},{... | collective-permute-start | bytes 393224 | tf_op jit(solution)/shard_map/ppermute | solution.py:16
  112.0 2.6 %fusion.65 = f32[4,16,128,128]{2,3,1,0:T(8,128)} fusion(bf16[128,4,128,1]{0,2,3,1:T(8,128)(2,1)S(1)} %copy.130, bf16[4,16,128,128]{2,3,1,0:T(8,128)(2,1)S(1)} %copy-done.18), kind=kOutput, calls=%fused_computation.112 | convolution fusion | flops 268435456 | bytes 6422528 | tf_op jit(solution)/shard_map/kgqs,skd->qkgd/dot_general | solution.py:53
  117.1 2.1 fusion.3
  125.0 4.1 %copy.116 = bf16[128,8192]{1,0:T(8,128)(2,1)} copy(bf16[128,8192]{0,1:T(8,128)(2,1)} %bitcast.190) | data formatting | bytes 4194304
  130.8 87.4 %all-reduce.4.cloned.1.call-done = (f32[8192,32]{0,1:T(8,128)}, f32[32,8192]{1,0:T(8,128)}) async-done(((f32[8192,32]{0,1:T(8,128)}, f32[32,8192]{1,0:T(8,128)}), (f32[8192,32]{0,1:T(8,128)}, f32[32,8192]{1,0:T(8,128)})) %all-reduce.4.cloned.1.call-update) | async-done | bytes 2097168 | tf_op jit(solution)/shard_map/psum | solution.py:182
  218.2 2.4 %copy.220 = f32[8192,32]{0,1:T(8,128)} copy(f32[8192,32]{0,1:T(8,128)} %get-tuple-element.52) | data formatting | bytes 2097152
  (129 shorter events, 43.9 us)
Async XLA Ops:
  7.2 17.1 %copy-start = (bf16[128,8192]{1,0:T(8,128)(2,1)S(1)}, bf16[128,8192]{1,0:T(8,128)(2,1)}, u32[]{:S(2)}) copy-start(bf16[128,8192]{1,0:T(8,128)(2,1)} %param.12) | copy-start | bytes 6291460
  7.2 211.0 %all-reduce.4.cloned.1.call-start = ((), (), s32[]{:S(2)}) async-start(), calls=%async_computation | async-start | bytes 4194304 | tf_op jit(solution)/shard_map/psum | solution.py:182
  9.2 20.8 %collective-permute-start.1 = (bf16[64,1024]{1,0:T(8,128)(2,1)S(1)}, bf16[64,1024]{1,0:T(8,128)(2,1)S(1)}, u32[]{:S(2)}, u32[]{:S(2)}) collective-permute-start(bf16[64,1024]{1,0:T(8,128)(2,1)S(1)} %get-tuple-element.31), channel_id=1, source_target_pairs={{2,0},{4,2},{6,4},{8,6},{10,8},{12,10},{14,12},{3,1},{5,3},{7,5},{... | collective-permute-start | bytes 393224 | tf_op jit(solution)/shard_map/ppermute | solution.py:16
  10.5 20.1 %collective-permute-start = (bf16[64,1024]{1,0:T(8,128)(2,1)S(1)}, bf16[64,1024]{1,0:T(8,128)(2,1)S(1)}, u32[]{:S(2)}, u32[]{:S(2)}) collective-permute-start(bf16[64,1024]{1,0:T(8,128)(2,1)S(1)} %get-tuple-element.32), channel_id=1, source_target_pairs={{0,2},{2,4},{4,6},{6,8},{8,10},{10,12},{12,14},{1,3},{3,5},{5,7},{... | collective-permute-start | bytes 393224 | tf_op jit(solution)/shard_map/ppermute | solution.py:16
  20.4 3.8 %copy-start.26 = (bf16[32,8192]{1,0:T(8,128)(2,1)S(1)}, bf16[32,8192]{1,0:T(8,128)(2,1)}, u32[]{:S(2)}) copy-start(bf16[32,8192]{1,0:T(8,128)(2,1)} %param.14) | copy-start | bytes 1572868
  30.7 3.4 %copy-start.3 = (bf16[16,8,64,128]{3,2,1,0:T(8,128)(2,1)S(1)}, bf16[16,8,64,128]{3,2,1,0:T(8,128)(2,1)}, u32[]{:S(2)}) copy-start(bf16[16,8,64,128]{3,2,1,0:T(8,128)(2,1)} %copy.165) | copy-start | bytes 6291460
  34.1 5.9 %copy-start.9 = (f32[4,16,128,64]{2,3,1,0:T(8,128)}, f32[4,16,128,64]{2,3,1,0:T(8,128)S(1)}, u32[]{:S(2)}) copy-start(f32[4,16,128,64]{2,3,1,0:T(8,128)S(1)} %get-tuple-element.42) | copy-start | bytes 6291460
  34.2 3.6 %copy-start.1 = (f32[4,128,128,16]{2,1,3,0:T(8,128)S(1)}, f32[4,128,128,16]{2,1,3,0:T(8,128)}, u32[]{:S(2)}) copy-start(f32[4,128,128,16]{2,1,3,0:T(8,128)} %get-tuple-element.46) | copy-start | bytes 12582916
  35.9 4.2 %copy-start.11 = (f32[4,16,128,64]{2,3,1,0:T(8,128)}, f32[4,16,128,64]{2,3,1,0:T(8,128)S(1)}, u32[]{:S(2)}) copy-start(f32[4,16,128,64]{2,3,1,0:T(8,128)S(1)} %get-tuple-element.44) | copy-start | bytes 6291460
  45.0 3.7 %copy-start.28 = (bf16[64,4,128]{2,1,0:T(4,128)(2,1)S(1)}, bf16[64,4,128]{2,1,0:T(4,128)(2,1)}, u32[]{:S(2)}) copy-start(bf16[64,4,128]{2,1,0:T(4,128)(2,1)} %reshape.326) | copy-start | bytes 196612
  51.4 5.6 %copy-start.27 = (bf16[128,4,128]{2,1,0:T(4,128)(2,1)S(1)}, bf16[128,4,128]{2,1,0:T(4,128)(2,1)}, u32[]{:S(2)}) copy-start(bf16[128,4,128]{2,1,0:T(4,128)(2,1)} %reshape.328) | copy-start | bytes 393220
  57.0 3.1 %copy-start.15 = (bf16[4,16,128,64]{2,3,1,0:T(8,128)(2,1)S(1)}, bf16[4,16,128,64]{2,3,1,0:T(8,128)(2,1)}, u32[]{:S(2)}) copy-start(bf16[4,16,128,64]{2,3,1,0:T(8,128)(2,1)} %get-tuple-element.37) | copy-start | bytes 3145732
  66.7 3.5 %copy-start.21 = (bf16[128,8192]{1,0:T(8,128)(2,1)S(1)}, bf16[128,8192]{1,0:T(8,128)(2,1)}, u32[]{:S(2)}) copy-start(bf16[128,8192]{1,0:T(8,128)(2,1)} %param.11) | copy-start | bytes 6291460
  77.5 3.3 %copy-start.12 = (f32[4,16,128,64]{2,3,1,0:T(8,128)S(1)}, f32[4,16,128,64]{2,3,1,0:T(8,128)}, u32[]{:S(2)}) copy-start(f32[4,16,128,64]{2,3,1,0:T(8,128)} %copy-done.11) | copy-start | bytes 6291460
  77.5 3.5 %copy-start.17 = (bf16[128,4,16,128]{0,3,2,1:T(8,128)(2,1)S(1)}, bf16[128,4,16,128]{0,3,2,1:T(8,128)(2,1)}, u32[]{:S(2)}) copy-start(bf16[128,4,16,128]{0,3,2,1:T(8,128)(2,1)} %copy.88) | copy-start | bytes 6291460
  84.5 4.6 %copy-start.31 = (f32[128,4,16]{0,2,1:T(8,128)S(1)}, f32[128,4,16]{0,2,1:T(8,128)}, u32[]{:S(2)}) copy-start(f32[128,4,16]{0,2,1:T(8,128)} %copy-done.30) | copy-start | bytes 98308
  89.1 5.7 %copy-start.32 = (bf16[128,32]{0,1:T(8,128)(2,1)S(1)}, bf16[128,32]{0,1:T(8,128)(2,1)}, u32[]{:S(2)}) copy-start(bf16[128,32]{0,1:T(8,128)(2,1)} %get-tuple-element.28) | copy-start | bytes 24580
  96.2 3.2 %copy-start.4 = (bf16[16,8,64,128]{3,2,1,0:T(8,128)(2,1)S(1)}, bf16[16,8,64,128]{3,2,1,0:T(8,128)(2,1)}, u32[]{:S(2)}) copy-start(bf16[16,8,64,128]{3,2,1,0:T(8,128)(2,1)} %copy.165) | copy-start | bytes 6291460
  96.2 6.7 %copy-start.16 = (bf16[4,16,128,64]{3,1,0,2:T(8,128)(2,1)S(1)}, bf16[4,16,128,64]{3,1,0,2:T(8,128)(2,1)}, u32[]{:S(2)}) copy-start(bf16[4,16,128,64]{3,1,0,2:T(8,128)(2,1)} %copy.114) | copy-start | bytes 3145732
  99.4 3.5 %copy-start.6 = (bf16[16,8,64,128]{3,2,1,0:T(8,128)(2,1)S(1)}, bf16[16,8,64,128]{3,2,1,0:T(8,128)(2,1)}, u32[]{:S(2)}) copy-start(bf16[16,8,64,128]{3,2,1,0:T(8,128)(2,1)} %copy.166) | copy-start | bytes 6291460
  101.5 27.5 %collective-permute-start.2 = (bf16[64,1024]{1,0:T(8,128)(2,1)}, bf16[64,1024]{1,0:T(8,128)(2,1)}, u32[]{:S(2)}, u32[]{:S(2)}) collective-permute-start(bf16[64,1024]{1,0:T(8,128)(2,1)} %pad_maximum_fusion), channel_id=1, source_target_pairs={{2,0},{4,2},{6,4},{8,6},{10,8},{12,10},{14,12},{3,1},{5,3},{7,5},{... | collective-permute-start | bytes 393224 | tf_op jit(solution)/shard_map/ppermute | solution.py:16
  103.8 8.2 %copy-start.18 = (bf16[4,16,128,128]{2,3,1,0:T(8,128)(2,1)S(1)}, bf16[4,16,128,128]{2,3,1,0:T(8,128)(2,1)}, u32[]{:S(2)}) copy-start(bf16[4,16,128,128]{2,3,1,0:T(8,128)(2,1)} %fusion.5) | copy-start | bytes 6291460
  105.9 23.2 %collective-permute-start.3 = (bf16[64,1024]{1,0:T(8,128)(2,1)}, bf16[64,1024]{1,0:T(8,128)(2,1)}, u32[]{:S(2)}, u32[]{:S(2)}) collective-permute-start(bf16[64,1024]{1,0:T(8,128)(2,1)} %pad_maximum_fusion.1), channel_id=1, source_target_pairs={{0,2},{2,4},{4,6},{6,8},{8,10},{10,12},{12,14},{1,3},{3,5},{5,7},{... | collective-permute-start | bytes 393224 | tf_op jit(solution)/shard_map/ppermute | solution.py:16
  117.1 3.0 %copy-start.22 = (bf16[4,16,128,128]{3,1,0,2:T(8,128)(2,1)S(1)}, bf16[4,16,128,128]{3,1,0,2:T(8,128)(2,1)}, u32[]{:S(2)}) copy-start(bf16[4,16,128,128]{3,1,0,2:T(8,128)(2,1)} %copy.105) | copy-start | bytes 6291460
  (14 other events, 29.3 us)
Sparse Core Ops, SparseCore 0:
  114.8 103.3 all-reduce.3
where the time goes:
time: 229 us; the launch traced here: 228 us
  waiting for transfers between devices  87.4 us (38%)
  local copies, waits for them, and re-layouts  48 us (21%)
  matrix products  46.8 us (20%)
  between operations  14.5 us (6%)
  starting transfers between devices  14.3 us (6%)
  other arithmetic  13.3 us (6%)
  blocking collectives  3.99 us (2%)
    psum x1, waiting for transfers between devices, shards(): lax.psum((down_adapter_gradient, up_adapter_gradient), 'ctx')  87.4 us
    unnamed x72, local copies, waits for them, and re-layouts  22.7 us
    ppermute x4, starting transfers between devices, passed_along(): return lax.ppermute(block, axis, route)  14.3 us
    convert_element_type x3, local copies, waits for them, and re-layouts, block_forward(): prob_low = prob_full.astype(jnp.bfloat16)  13 us
    dot_general x3, matrix products, block_backward(): jnp.einsum('qkgd,skd->kgqs', heads_grad, values_here, preferred_element_t...  9.19 us
    dot_general x3, matrix products, block_scores(): jnp.einsum('qkgd,skd->kgqs', queries, keys_here, preferred_element_type=j...  9.1 us
    dot_general x3, matrix products, block_forward(): jnp.einsum('kgqs,skd->qkgd', prob_low, values_here, preferred_element_typ...  5.97 us
    dot_general x3, matrix products, block_backward(): jnp.einsum('kgqs,skd->qkgd', dscores, keys_here, preferred_element_type=j...  5.54 us
  transfers between devices with their start and end apart: 5, of which 1 were waited for; matrix products, arithmetic and copies ran while one was open for 14% of the time, Pallas kernels for 0%

commit v1 on v0

v1 whole, which is shorter than its diff:
```python
import functools

import jax
import jax.numpy as jnp
from jax import lax
from jax.experimental import pallas as pl
from jax.experimental.pallas import tpu as pltpu
from jax.sharding import PartitionSpec as P

HEAD_SIZE = 128
NEG = -1e30
ADAPTER_SCALE = 0.5
MESH = pl.DeviceIdType.MESH
F32 = jnp.float32
BF16 = jnp.bfloat16


def dot(a, b, contract):
    return lax.dot_general(a, b, (contract, ((), ())), preferred_element_type=F32)


def nn(a, b):
    return dot(a, b, ((1,), (0,)))


def nt(a, b):
    return dot(a, b, ((1,), (1,)))


def tn(a, b):
    return dot(a, b, ((0,), (0,)))


def kernel(
    ctx_size, query_hbm, key_hbm, value_hbm, upstream_hbm, grad_hbm, down_hbm, up_hbm, lengths_ref,
    dquery_hbm, dkey_ref, dvalue_ref, ddown_ref, dup_ref,
    query, upstream, grad, down, up, keys, values, bias, probs, attn, dquery,
    low_send, low_recv, low, low_t, outer_send, outer_recv,
    own_dkv, back_send, back_recv, acc, part_send, part_recv, total,
    load_sem, store_sem, halo_send_sem, halo_recv_sem, low_sem, back_sem, step_send_sem, step_recv_sem,
):
    rows, width = query.shape
    half = rows // 2
    kv_width = keys.shape[2]
    kv_heads = kv_width // HEAD_SIZE
    group = width // kv_width
    group_width = group * HEAD_SIZE
    scale = HEAD_SIZE ** (-0.5)
    levels = ctx_size.bit_length() - 1
    me = lax.axis_index("ctx")
    tp = lax.axis_index("tp")
    first = me == 0
    last = me == ctx_size - 1
    bits = [(me // (1 << b)) % 2 for b in range(levels)]
    partners = [me + (1 << b) * (1 - 2 * bits[b]) for b in range(levels)]
    orders = [list(range(levels)), list(range(levels))]
    for i in range(0, levels - 1, 2):
        orders[0][i], orders[0][i + 1] = i + 1, i

    loads = []
    for i, (src, dst) in enumerate(
        [
            (grad_hbm, grad),
            (up_hbm, up),
            (query_hbm, query),
            (key_hbm.at[0:half], keys.at[0, half:rows]),
            (key_hbm.at[half:rows], keys.at[1, half:rows]),
            (value_hbm.at[0:half], values.at[0, half:rows]),
            (value_hbm.at[half:rows], values.at[1, half:rows]),
            (down_hbm, down),
            (upstream_hbm, upstream),
        ]
    ):
        copy = pltpu.make_async_copy(src, dst, load_sem.at[i])
        copy.start()
        loads.append(copy)

    barrier = pltpu.get_barrier_semaphore()
    pl.semaphore_signal(barrier, inc=1, device_id={"tp": 1 - tp}, device_id_type=MESH)
    for partner in partners:
        pl.semaphore_signal(barrier, inc=1, device_id={"ctx": partner}, device_id_type=MESH)

    @pl.when(jnp.logical_not(first))
    def _():
        pl.semaphore_signal(barrier, inc=1, device_id={"ctx": me - 1}, device_id_type=MESH)

    @pl.when(jnp.logical_not(last))
    def _():
        pl.semaphore_signal(barrier, inc=1, device_id={"ctx": me + 1}, device_id_type=MESH)

    lengths = lengths_ref[...].astype(F32)
    docs = lengths.shape[1]
    line = lax.broadcasted_iota(jnp.int32, (docs, docs), 0)
    column = lax.broadcasted_iota(jnp.int32, (docs, docs), 1)
    tall = jnp.sum(jnp.where(line == column, lengths, 0.0), axis=1, keepdims=True)
    starts = jnp.sum(jnp.where(line < column, tall, 0.0), axis=0, keepdims=True)
    for t in range(2):
        stretch = me if t == 0 else 2 * ctx_size - 1 - me
        spot = (lax.broadcasted_iota(jnp.int32, (half, 1), 0) + stretch * half).astype(F32)
        begin = jnp.max(jnp.where(starts <= spot, starts, -1.0), axis=1, keepdims=True)
        key_spot = (
            lax.broadcasted_iota(jnp.int32, (half, rows), 1) + (stretch - 1) * half
        ).astype(F32)
        allowed = jnp.logical_and(key_spot >= begin, key_spot <= spot)
        bias[t] = jnp.where(allowed, 0.0, NEG)

    pl.semaphore_wait(
        barrier, 1 + levels + jnp.where(first, 0, 1) + jnp.where(last, 0, 1)
    )

    def halo(hbm, buffer, which, t):
        part = hbm.at[0:half] if t == 0 else hbm.at[half:rows]
        target = me + 1 if t == 0 else me - 1
        return pltpu.make_async_remote_copy(
            src_ref=part,
            dst_ref=buffer.at[t, 0:half],
            send_sem=halo_send_sem.at[which, t],
            recv_sem=halo_recv_sem.at[which, t],
            device_id={"ctx": target},
            device_id_type=MESH,
        )

    halos = [halo(key_hbm, keys, 0, t) for t in range(2)] + [
        halo(value_hbm, values, 1, t) for t in range(2)
    ]

    @pl.when(jnp.logical_not(last))
    def _():
        halos[0].start()
        halos[2].start()

    @pl.when(jnp.logical_not(first))
    def _():
        halos[1].start()
        halos[3].start()

    loads[0].wait()
    loads[1].wait()
    low_send[...] = nt(grad[...], up[...]).T
    low_copy = pltpu.make_async_remote_copy(
        src_ref=low_send, dst_ref=low_recv, send_sem=low_sem.at[0], recv_sem=low_sem.at[1],
        device_id={"tp": 1 - tp}, device_id_type=MESH,
    )
    low_copy.start()

    for i in range(2, 8):
        loads[i].wait()

    @pl.when(first)
    def _():
        keys[0, 0:half] = jnp.zeros((half, kv_width), BF16)
        values[0, 0:half] = jnp.zeros((half, kv_width), BF16)

    @pl.when(jnp.logical_not(first))
    def _():
        halos[0].wait_recv()
        halos[2].wait_recv()

    @pl.when(last)
    def _():
        keys[1, 0:half] = keys[0, half:rows]
        values[1, 0:half] = values[0, half:rows]

    @pl.when(jnp.logical_not(last))
    def _():
        halos[1].wait_recv()
        halos[3].wait_recv()

    def stacked(ref, t, g):
        return jnp.concatenate(
            [
                ref[t * half : (t + 1) * half, g * group_width + h * HEAD_SIZE : g * group_width + (h + 1) * HEAD_SIZE]
                for h in range(group)
            ],
            axis=0,
        )

    def unstack(ref, t, g, block):
        for h in range(group):
            start = g * group_width + h * HEAD_SIZE
            ref[t * half : (t + 1) * half, start : start + HEAD_SIZE] = block[h * half : (h + 1) * half]

    outer = jnp.zeros((rows, low_send.shape[0]), F32)
    for g in range(kv_heads):
        head = slice(g * HEAD_SIZE, (g + 1) * HEAD_SIZE)
        for t in range(2):
            scores = nt(stacked(query, t, g), keys[t, :, head]) * scale
            scores = scores.reshape(group, half, rows) + bias[t][None]
            scores = scores.reshape(group * half, rows)
            expo = jnp.exp(scores - jnp.max(scores, axis=1, keepdims=True))
            prob = expo * (1.0 / jnp.sum(expo, axis=1, keepdims=True))
            probs[2 * g + t] = prob
            out = nn(prob.astype(BF16), values[t, :, head]).astype(BF16)
            unstack(attn, t, g, out)
        columns = slice(g * group_width, (g + 1) * group_width)
        outer = outer + nt(attn[:, columns], down[:, columns])
    outer_send[...] = outer.T
    outer_copy = pltpu.make_async_remote_copy(
        src_ref=outer_send, dst_ref=outer_recv, send_sem=low_sem.at[2], recv_sem=low_sem.at[3],
        device_id={"tp": 1 - tp}, device_id_type=MESH,
    )
    outer_copy.start()

    slot_width = acc.shape[3]
    started = []

    def ranges(which):
        bases = [0]
        for s in range(levels):
            bases.append(bases[-1] + bits[orders[which][s]] * (ctx_size >> (s + 1)))
        return bases

    bases = [ranges(0), ranges(1)]

    def begin_step(which, step):
        if step < levels:
            s = step
            size = ctx_size >> (s + 1)
            bit = bits[orders[which][s]]
            away = bases[which][s] + (1 - bit) * size
            part_send[which, pl.ds(away, size)] = acc[which, pl.ds(away, size)].astype(BF16)
            src = part_send.at[which, pl.ds(away, size)]
            offset = ctx_size - (ctx_size >> s)
            dst = part_recv.at[which, pl.ds(offset, size)]
        else:
            s = 2 * levels - 1 - step
            size = ctx_size >> (s + 1)
            if step == levels:
                mine = bases[which][levels]
                total[which, pl.ds(mine, 1)] = acc[which, pl.ds(mine, 1)].astype(BF16)
            src = total.at[which, pl.ds(bases[which][s + 1], size)]
            dst = src
        copy = pltpu.make_async_remote_copy(
            src_ref=src, dst_ref=dst,
            send_sem=step_send_sem.at[which, step], recv_sem=step_recv_sem.at[which, step],
            device_id={"ctx": partners[orders[which][s]]}, device_id_type=MESH,
        )
        copy.start()
        started.append(copy)
        return copy

    def end_step(which, step, copy):
        copy.wait_recv()
        if step < levels:
            size = ctx_size >> (step + 1)
            offset = ctx_size - (ctx_size >> step)
            keep = pl.ds(bases[which][step + 1], size)
            acc[which, keep] = acc[which, keep] + part_recv[which, pl.ds(offset, size)].astype(F32)

    low_copy.wait_recv()
    low_sum = (low_send[...] + low_recv[...]).astype(BF16)
    low_t[...] = low_sum
    low[...] = (low_send[...] + low_recv[...]).T.astype(BF16)
    for i in range(ctx_size):
        acc[0, i] = ADAPTER_SCALE * nn(low_sum, attn[:, i * slot_width : (i + 1) * slot_width])
    flying = [begin_step(0, 0)]
    outer_copy.wait_recv()
    outer_sum = (outer_send[...] + outer_recv[...]).astype(BF16)
    for i in range(ctx_size):
        acc[1, i] = ADAPTER_SCALE * nn(outer_sum, grad[:, i * slot_width : (i + 1) * slot_width])
    flying.append(begin_step(1, 0))
    loads[8].wait()

    stores = []

    def backward(g):
        head = slice(g * HEAD_SIZE, (g + 1) * HEAD_SIZE)
        tail = slice(kv_width + g * HEAD_SIZE, kv_width + (g + 1) * HEAD_SIZE)
        columns = slice(g * group_width, (g + 1) * group_width)
        upstream[:, columns] = (
            upstream[:, columns].astype(F32) + ADAPTER_SCALE * nn(low[...], down[:, columns])
        ).astype(BF16)
        for t in range(2):
            dout = stacked(upstream, t, g)
            out = stacked(attn, t, g)
            delta = jnp.sum(dout.astype(F32) * out.astype(F32), axis=1, keepdims=True)
            prob = probs[2 * g + t]
            dscores = (prob * (nt(dout, values[t, :, head]) - delta)).astype(BF16)
            dq = (nn(dscores, keys[t, :, head]) * scale).astype(BF16)
            unstack(dquery, t, g, dq)
            dk = tn(dscores, stacked(query, t, g)) * scale
            dv = tn(prob.astype(BF16), dout)
            back_send[t, :, head] = dk[0:half].astype(BF16)
            back_send[t, :, tail] = dv[0:half].astype(BF16)
            own_dkv[t, :, head] = dk[half:rows]
            own_dkv[t, :, tail] = dv[half:rows]
        store = pltpu.make_async_copy(
            dquery.at[:, columns], dquery_hbm.at[:, columns], store_sem.at[g]
        )
        store.start()
        stores.append(store)

    backs = []

    def send_back():
        for t in range(2):
            backs.append(
                pltpu.make_async_remote_copy(
                    src_ref=back_send.at[t], dst_ref=back_recv.at[t],
                    send_sem=back_sem.at[0, t], recv_sem=back_sem.at[1, t],
                    device_id={"ctx": me - 1 if t == 0 else me + 1}, device_id_type=MESH,
                )
            )

        @pl.when(jnp.logical_not(first))
        def _():
            backs[0].start()

        @pl.when(jnp.logical_not(last))
        def _():
            backs[1].start()

        @pl.when(first)
        def _():
            back_recv[1] = jnp.zeros(back_recv.shape[1:], BF16)

        @pl.when(last)
        def _():
            back_recv[0] = back_send[1]

    for step in range(2 * levels):
        if step < kv_heads:
            backward(step)
            if step == kv_heads - 1:
                send_back()
        for which in range(2):
            end_step(which, step, flying[which])
            if step + 1 < 2 * levels:
                flying[which] = begin_step(which, step + 1)
    for g in range(2 * levels, kv_heads):
        backward(g)
    if kv_heads > 2 * levels:
        send_back()

    for i in range(ctx_size):
        columns = slice(i * slot_width, (i + 1) * slot_width)
        ddown_ref[:, columns] = total[0, i].astype(F32)
        dup_ref[:, columns] = total[1, i].astype(F32)

    @pl.when(jnp.logical_not(last))
    def _():
        backs[0].wait_recv()

    @pl.when(jnp.logical_not(first))
    def _():
        backs[1].wait_recv()

    for t in range(2):
        both = own_dkv[t] + back_recv[t].astype(F32)
        dkey_ref[t * half : (t + 1) * half] = both[:, :kv_width].astype(BF16)
        dvalue_ref[t * half : (t + 1) * half] = both[:, kv_width:].astype(BF16)

    for store in stores:
        store.wait()
    for copy in started:
        copy.wait_send()
    low_copy.wait_send()
    outer_copy.wait_send()

    @pl.when(jnp.logical_not(last))
    def _():
        halos[0].wait_send()
        halos[2].wait_send()
        backs[1].wait_send()

    @pl.when(jnp.logical_not(first))
    def _():
        halos[1].wait_send()
        halos[3].wait_send()
        backs[0].wait_send()


def shards(
    query,
    key_input,
    value,
    upstream,
    output_gradient,
    down_adapter,
    up_adapter,
    document_length_list,
):
    rows, width = query.shape
    kv_width = key_input.shape[1]
    kv_heads = kv_width // HEAD_SIZE
    group = width // kv_width
    rank, model = up_adapter.shape
    half = rows // 2
    ctx_size = lax.axis_size("ctx")
    levels = ctx_size.bit_length() - 1
    slot = (ctx_size, rank, width // ctx_size)
    anywhere = pl.BlockSpec(memory_space=pl.ANY)
    vmem = pl.BlockSpec(memory_space=pltpu.VMEM)
    dma = pltpu.SemaphoreType.DMA
    outs = pl.pallas_call(
        functools.partial(kernel, ctx_size),
        out_shape=(
            jax.ShapeDtypeStruct((rows, width), BF16),
            jax.ShapeDtypeStruct((rows, kv_width), BF16),
            jax.ShapeDtypeStruct((rows, kv_width), BF16),
            jax.ShapeDtypeStruct((rank, width), F32),
            jax.ShapeDtypeStruct((rank, model), F32),
        ),
        in_specs=[anywhere] * 7 + [vmem],
        out_specs=(anywhere, vmem, vmem, vmem, vmem),
        scratch_shapes=[
            pltpu.VMEM((rows, width), BF16),
            pltpu.VMEM((rows, width), BF16),
            pltpu.VMEM((rows, model), BF16),
            pltpu.VMEM((rank, width), BF16),
            pltpu.VMEM((rank, model), BF16),
            pltpu.VMEM((2, rows, kv_width), BF16),
            pltpu.VMEM((2, rows, kv_width), BF16),
            pltpu.VMEM((2, half, rows), F32),
            pltpu.VMEM((2 * kv_heads, group * half, rows), F32),
            pltpu.VMEM((rows, width), BF16),
            pltpu.VMEM((rows, width), BF16),
            pltpu.VMEM((rank, rows), F32),
            pltpu.VMEM((rank, rows), F32),
            pltpu.VMEM((rows, rank), BF16),
            pltpu.VMEM((rank, rows), BF16),
            pltpu.VMEM((rank, rows), F32),
            pltpu.VMEM((rank, rows), F32),
            pltpu.VMEM((2, half, 2 * kv_width), F32),
            pltpu.VMEM((2, half, 2 * kv_width), BF16),
            pltpu.VMEM((2, half, 2 * kv_width), BF16),
            pltpu.VMEM((2,) + slot, F32),
            pltpu.VMEM((2,) + slot, BF16),
            pltpu.VMEM((2,) + slot, BF16),
            pltpu.VMEM((2,) + slot, BF16),
            dma((9,)),
            dma((kv_heads,)),
            dma((2, 2)),
            dma((2, 2)),
            dma((4,)),
            dma((2, 2)),
            dma((2, 2 * levels)),
            dma((2, 2 * levels)),
        ],
        compiler_params=pltpu.CompilerParams(
            collective_id=0, has_side_effects=True, vmem_limit_bytes=48 * 1024 * 1024
        ),
    )(
        query, key_input, value, upstream, output_gradient, down_adapter.T, up_adapter,
        document_length_list[None, :],
    )
    dquery, dkey, dvalue, ddown, dup = outs
    return dquery, dkey, dvalue, ddown.T, dup


def solution(mesh):
    in_specs = (
        P(("groups", "ctx"), "tp"),
        P(("groups", "ctx"), "tp"),
        P(("groups", "ctx"), "tp"),
        P(("groups", "ctx"), "tp"),
        P(("groups", "ctx"), "tp"),
        P("tp", None),
        P(None, "tp"),
        P("groups"),
    )
    out_specs = (
        P(("groups", "ctx"), "tp"),
        P(("groups", "ctx"), "tp"),
        P(("groups", "ctx"), "tp"),
        P(("groups", "tp"), None),
        P("groups", "tp"),
    )
    return jax.shard_map(shards, mesh=mesh, in_specs=in_specs, out_specs=out_specs, check_vma=False)
```

time: 229 us -> 64.5 us (0.28)
  waiting for transfers between devices: 87.4 us -> 0 us
  Pallas kernels: 0 us -> 54.5 us
  matrix products: 46.8 us -> 0 us
  local copies, waits for them, and re-layouts: 48 us -> 9.11 us
  starting transfers between devices: 14.3 us -> 0 us
  between operations: 14.5 us -> 0.66 us
  other arithmetic: 13.3 us -> 0 us
  blocking collectives: 3.99 us -> 0 us
    psum x1 -> x0, waiting for transfers between devices: 87.4 us -> none  [shards(): lax.psum((down_adapter_gradient, up_adapter_gradient), 'ctx')]
    pallas_call x0 -> x1, Pallas kernels: none -> 54.5 us  [shards(): pl.pallas_call(functools.partial(kernel, ctx_size), out_shape=(jax.ShapeD...]
    dot_general x23 -> x0, matrix products: 46.8 us -> none  [the longest x3 9.19 us: block_backward(): jnp.einsum('qkgd,skd->kgqs', heads_grad, values_here, preferred_element_t...]
    ppermute x4 -> x0, starting transfers between devices: 14.3 us -> none  [passed_along(): return lax.ppermute(block, axis, route)]
    unnamed x72 -> x15, local copies, waits for them, and re-layouts: 22.7 us -> 9.11 us
    convert_element_type x3 -> x0, local copies, waits for them, and re-layouts: 13 us -> none  [block_forward(): prob_low = prob_full.astype(jnp.bfloat16)]
    reshape x14 -> x0, local copies, waits for them, and re-layouts: 9.09 us -> none  [the longest x1 4.53 us: shards(): heads_grad = attention_gradient.reshape(head_shape)]
    reduce_sum x4 -> x0, other arithmetic: 5.55 us -> none  [the longest x1 3.24 us: shards(): jnp.sum(heads_grad.astype(jnp.float32) * attn_out.astype(jnp.float32), ax...]
  transfers between devices with their start and end apart: 5 -> 0, of which waited for: 1 -> 0; matrix products, arithmetic and copies ran while one was open for 14% -> 0% of each run, Pallas kernels for 0% -> 0%
where the time goes in v1:
time: 64.5 us; the launch traced here: 64.3 us
  Pallas kernels  54.5 us (84%)
  local copies, waits for them, and re-layouts  9.11 us (14%)
  between operations  0.66 us (1%)
    pallas_call x1, Pallas kernels, shards(): pl.pallas_call(functools.partial(kernel, ctx_size), out_shape=(jax.ShapeD...  54.5 us
    unnamed x15, local copies, waits for them, and re-layouts  9.11 us

profile of v1, /device:TPU:0, one launch (start us, length us, event | category | flops | bytes accessed | tf_op | source)
XLA Modules:
  0.0 64.3 jit_solution(8504689232311013271)
XLA Ops:
  0.6 0.0 copy-start
  0.6 1.0 %copy-done = bf16[8192,32]{0,1:T(8,128)(2,1)S(1)} copy-done((bf16[8192,32]{0,1:T(8,128)(2,1)S(1)}, bf16[8192,32]{0,1:T(8,128)(2,1)}, u32[]{:S(2)}) %copy-start) | copy-done | bytes 524312
  1.7 0.0 copy-start.1
  1.7 1.0 %copy-done.1 = bf16[32,8192]{1,0:T(8,128)(2,1)S(1)} copy-done((bf16[32,8192]{1,0:T(8,128)(2,1)S(1)}, bf16[32,8192]{1,0:T(8,128)(2,1)}, u32[]{:S(2)}) %copy-start.1) | copy-done | bytes 524312
  2.7 0.0 copy-start.2
  2.7 0.9 %copy-done.2 = bf16[128,512]{1,0:T(8,128)(2,1)S(1)} copy-done((bf16[128,512]{1,0:T(8,128)(2,1)S(1)}, bf16[128,512]{1,0:T(8,128)(2,1)}, u32[]{:S(2)}) %copy-start.2) | copy-done | bytes 131096
  3.6 0.0 copy-start.3
  3.6 0.9 %copy-done.3 = bf16[128,512]{1,0:T(8,128)(2,1)S(1)} copy-done((bf16[128,512]{1,0:T(8,128)(2,1)S(1)}, bf16[128,512]{1,0:T(8,128)(2,1)}, u32[]{:S(2)}) %copy-start.3) | copy-done | bytes 131096
  4.5 0.0 copy-start.4
  4.5 0.7 %copy-done.4 = s32[32]{0:T(128)S(1)} copy-done((s32[32]{0:T(128)S(1)}, s32[32]{0:T(128)}, u32[]{:S(2)}) %copy-start.4) | copy-done | bytes 152
  5.2 54.5 %shard_map.119 = (bf16[128,8192]{1,0:T(8,128)(2,1)S(1)}, bf16[128,512]{1,0:T(8,128)(2,1)S(1)}, bf16[128,512]{1,0:T(8,128)(2,1)S(1)}, f32[32,8192]{1,0:T(8,128)S(1)}, f32[32,8192]{1,0:T(8,128)S(1)}) custom-call(bf16[128,8192]{1,0:T(8,128)(2,1)} %query_hbm.1, bf16[128,512]{1,0:T(8,128)(2,1)S(1)} %copy-done.2, bf16[128,512]{1,0:T(8,128)(2,1)S(1)} %copy-done.3, ...), custom_call_target="tpu_custom_call" | custom-call | tf_op jit(solution)/shard_map/pallas_call | solution.py:395
  59.7 1.3 %copy.18 = bf16[128,8192]{1,0:T(8,128)(2,1)} copy(bf16[128,8192]{1,0:T(8,128)(2,1)S(1)} %get-tuple-element.20) | data formatting | bytes 4194304
  61.0 0.7 %copy.19 = bf16[128,512]{1,0:T(8,128)(2,1)} copy(bf16[128,512]{1,0:T(8,128)(2,1)S(1)} %get-tuple-element.21) | data formatting | bytes 262144
  61.7 0.7 %copy.20 = bf16[128,512]{1,0:T(8,128)(2,1)} copy(bf16[128,512]{1,0:T(8,128)(2,1)S(1)} %get-tuple-element.22) | data formatting | bytes 262144
  62.4 1.0 %copy.21 = f32[8192,32]{0,1:T(8,128)} copy(f32[8192,32]{0,1:T(8,128)S(1)} %bitcast.3) | data formatting | bytes 2097152
  63.3 1.0 %copy.22 = f32[32,8192]{1,0:T(8,128)} copy(f32[32,8192]{1,0:T(8,128)S(1)} %get-tuple-element.24) | data formatting | bytes 2097152
Async XLA Ops:
  0.6 1.0 %copy-start = (bf16[8192,32]{0,1:T(8,128)(2,1)S(1)}, bf16[8192,32]{0,1:T(8,128)(2,1)}, u32[]{:S(2)}) copy-start(bf16[8192,32]{0,1:T(8,128)(2,1)} %param.13) | copy-start | bytes 1572868
  1.7 1.0 %copy-start.1 = (bf16[32,8192]{1,0:T(8,128)(2,1)S(1)}, bf16[32,8192]{1,0:T(8,128)(2,1)}, u32[]{:S(2)}) copy-start(bf16[32,8192]{1,0:T(8,128)(2,1)} %up_hbm.1) | copy-start | bytes 1572868
  2.7 0.9 %copy-start.2 = (bf16[128,512]{1,0:T(8,128)(2,1)S(1)}, bf16[128,512]{1,0:T(8,128)(2,1)}, u32[]{:S(2)}) copy-start(bf16[128,512]{1,0:T(8,128)(2,1)} %key_hbm.1) | copy-start | bytes 393220
  3.6 0.9 %copy-start.3 = (bf16[128,512]{1,0:T(8,128)(2,1)S(1)}, bf16[128,512]{1,0:T(8,128)(2,1)}, u32[]{:S(2)}) copy-start(bf16[128,512]{1,0:T(8,128)(2,1)} %value_hbm.1) | copy-start | bytes 393220
  4.5 0.7 %copy-start.4 = (s32[32]{0:T(128)S(1)}, s32[32]{0:T(128)}, u32[]{:S(2)}) copy-start(s32[32]{0:T(128)} %param.15) | copy-start | bytes 388

commit v2 on v1

--- a/solution.py
+++ b/solution.py
@@ -32,11 +32,11 @@
 
 
 def kernel(
-    ctx_size, query_hbm, key_hbm, value_hbm, upstream_hbm, grad_hbm, down_hbm, up_hbm, lengths_ref,
-    dquery_hbm, dkey_ref, dvalue_ref, ddown_ref, dup_ref,
+    ctx_size, query_hbm, key_hbm, value_hbm, upstream_hbm, grad_hbm, down_hbm, up_hbm, lengths_hbm,
+    dquery_hbm, dkey_ref, dvalue_ref, total,
     query, upstream, grad, down, up, keys, values, bias, probs, attn, dquery,
-    low_send, low_recv, low, low_t, outer_send, outer_recv,
-    own_dkv, back_send, back_recv, acc, part_send, part_recv, total,
+    low_send, low_recv, low, outer_send, outer_recv,
+    own_dkv, back_send, back_recv, acc, part_send, part_recv, lengths_vmem,
     load_sem, store_sem, halo_send_sem, halo_recv_sem, low_sem, back_sem, step_send_sem, step_recv_sem,
 ):
     rows, width = query.shape
@@ -53,9 +53,14 @@
     last = me == ctx_size - 1
     bits = [(me // (1 << b)) % 2 for b in range(levels)]
     partners = [me + (1 << b) * (1 - 2 * bits[b]) for b in range(levels)]
-    orders = [list(range(levels)), list(range(levels))]
+    cuts = acc.shape[0] // 2
+    swapped = list(range(levels))
     for i in range(0, levels - 1, 2):
-        orders[0][i], orders[0][i + 1] = i + 1, i
+        swapped[i], swapped[i + 1] = i + 1, i
+    orders = [
+        swapped if w < cuts and w % 2 == 0 or w == cuts + 1 else list(range(levels))
+        for w in range(2 * cuts)
+    ]
 
     loads = []
     for i, (src, dst) in enumerate(
@@ -69,6 +74,7 @@
             (value_hbm.at[half:rows], values.at[1, half:rows]),
             (down_hbm, down),
             (upstream_hbm, upstream),
+            (lengths_hbm, lengths_vmem),
         ]
     ):
         copy = pltpu.make_async_copy(src, dst, load_sem.at[i])
@@ -88,7 +94,8 @@
     def _():
         pl.semaphore_signal(barrier, inc=1, device_id={"ctx": me + 1}, device_id_type=MESH)
 
-    lengths = lengths_ref[...].astype(F32)
+    loads[9].wait()
+    lengths = lengths_vmem[...].astype(F32)
     docs = lengths.shape[1]
     line = lax.broadcasted_iota(jnp.int32, (docs, docs), 0)
     column = lax.broadcasted_iota(jnp.int32, (docs, docs), 1)
@@ -180,37 +187,20 @@
             start = g * group_width + h * HEAD_SIZE
             ref[t * half : (t + 1) * half, start : start + HEAD_SIZE] = block[h * half : (h + 1) * half]
 
-    outer = jnp.zeros((rows, low_send.shape[0]), F32)
-    for g in range(kv_heads):
-        head = slice(g * HEAD_SIZE, (g + 1) * HEAD_SIZE)
-        for t in range(2):
-            scores = nt(stacked(query, t, g), keys[t, :, head]) * scale
-            scores = scores.reshape(group, half, rows) + bias[t][None]
-            scores = scores.reshape(group * half, rows)
-            expo = jnp.exp(scores - jnp.max(scores, axis=1, keepdims=True))
-            prob = expo * (1.0 / jnp.sum(expo, axis=1, keepdims=True))
-            probs[2 * g + t] = prob
-            out = nn(prob.astype(BF16), values[t, :, head]).astype(BF16)
-            unstack(attn, t, g, out)
-        columns = slice(g * group_width, (g + 1) * group_width)
-        outer = outer + nt(attn[:, columns], down[:, columns])
-    outer_send[...] = outer.T
-    outer_copy = pltpu.make_async_remote_copy(
-        src_ref=outer_send, dst_ref=outer_recv, send_sem=low_sem.at[2], recv_sem=low_sem.at[3],
-        device_id={"tp": 1 - tp}, device_id_type=MESH,
-    )
-    outer_copy.start()
+    low_copy.wait_recv()
+    low_t = (low_send[...] + low_recv[...]).astype(BF16)
+    low[...] = (low_send[...] + low_recv[...]).T.astype(BF16)
 
     slot_width = acc.shape[3]
     started = []
 
-    def ranges(which):
+    def ranges(order):
         bases = [0]
         for s in range(levels):
-            bases.append(bases[-1] + bits[orders[which][s]] * (ctx_size >> (s + 1)))
+            bases.append(bases[-1] + bits[order[s]] * (ctx_size >> (s + 1)))
         return bases
 
-    bases = [ranges(0), ranges(1)]
+    bases = [ranges(order) for order in orders]
 
     def begin_step(which, step):
         if step < levels:
@@ -247,48 +237,79 @@
             keep = pl.ds(bases[which][step + 1], size)
             acc[which, keep] = acc[which, keep] + part_recv[which, pl.ds(offset, size)].astype(F32)
 
-    low_copy.wait_recv()
-    low_sum = (low_send[...] + low_recv[...]).astype(BF16)
-    low_t[...] = low_sum
-    low[...] = (low_send[...] + low_recv[...]).T.astype(BF16)
-    for i in range(ctx_size):
-        acc[0, i] = ADAPTER_SCALE * nn(low_sum, attn[:, i * slot_width : (i + 1) * slot_width])
-    flying = [begin_step(0, 0)]
+    flying = [None] * (2 * cuts)
+    events = [(step, which) for step in range(2 * levels) for which in range(2 * cuts)]
+
+    def advance(step, which):
+        end_step(which, step, flying[which])
+        if step + 1 < 2 * levels:
+            flying[which] = begin_step(which, step + 1)
+
+    def fill(which, left, right):
+        for i in range(ctx_size):
+            start = ((which % cuts) * ctx_size + i) * slot_width
+            acc[which, i] = ADAPTER_SCALE * nn(left, right[:, start : start + slot_width])
+        flying[which] = begin_step(which, 0)
+
+    outer = jnp.zeros((rows, low_send.shape[0]), F32)
+    for g in range(kv_heads):
+        head = slice(g * HEAD_SIZE, (g + 1) * HEAD_SIZE)
+        for t in range(2):
+            scores = nt(stacked(query, t, g), keys[t, :, head]) * scale
+            scores = scores.reshape(group, half, rows) + bias[t][None]
+            scores = scores.reshape(group * half, rows)
+            expo = jnp.exp(scores - jnp.max(scores, axis=1, keepdims=True))
+            prob = expo * (1.0 / jnp.sum(expo, axis=1, keepdims=True))
+            probs[2 * g + t] = prob
+            out = nn(prob.astype(BF16), values[t, :, head]).astype(BF16)
+            unstack(attn, t, g, out)
+        columns = slice(g * group_width, (g + 1) * group_width)
+        outer = outer + nt(attn[:, columns], down[:, columns])
+        if g == kv_heads - 1:
+            outer_send[...] = outer.T
+            outer_copy = pltpu.make_async_remote_copy(
+                src_ref=outer_send, dst_ref=outer_recv, send_sem=low_sem.at[2], recv_sem=low_sem.at[3],
+                device_id={"tp": 1 - tp}, device_id_type=MESH,
+            )
+            outer_copy.start()
+        for which in range(cuts):
+            if (which + 1) * kv_heads // cuts == g + 1:
+                fill(which, low_t, attn)
     outer_copy.wait_recv()
     outer_sum = (outer_send[...] + outer_recv[...]).astype(BF16)
-    for i in range(ctx_size):
-        acc[1, i] = ADAPTER_SCALE * nn(outer_sum, grad[:, i * slot_width : (i + 1) * slot_width])
-    flying.append(begin_step(1, 0))
+    for which in range(cuts):
+        fill(cuts + which, outer_sum, grad)
     loads[8].wait()
 
     stores = []
 
-    def backward(g):
+    def backward(g, t):
         head = slice(g * HEAD_SIZE, (g + 1) * HEAD_SIZE)
         tail = slice(kv_width + g * HEAD_SIZE, kv_width + (g + 1) * HEAD_SIZE)
         columns = slice(g * group_width, (g + 1) * group_width)
-        upstream[:, columns] = (
-            upstream[:, columns].astype(F32) + ADAPTER_SCALE * nn(low[...], down[:, columns])
-        ).astype(BF16)
-        for t in range(2):
-            dout = stacked(upstream, t, g)
-            out = stacked(attn, t, g)
-            delta = jnp.sum(dout.astype(F32) * out.astype(F32), axis=1, keepdims=True)
-            prob = probs[2 * g + t]
-            dscores = (prob * (nt(dout, values[t, :, head]) - delta)).astype(BF16)
-            dq = (nn(dscores, keys[t, :, head]) * scale).astype(BF16)
-            unstack(dquery, t, g, dq)
-            dk = tn(dscores, stacked(query, t, g)) * scale
-            dv = tn(prob.astype(BF16), dout)
-            back_send[t, :, head] = dk[0:half].astype(BF16)
-            back_send[t, :, tail] = dv[0:half].astype(BF16)
-            own_dkv[t, :, head] = dk[half:rows]
-            own_dkv[t, :, tail] = dv[half:rows]
-        store = pltpu.make_async_copy(
-            dquery.at[:, columns], dquery_hbm.at[:, columns], store_sem.at[g]
-        )
-        store.start()
-        stores.append(store)
+        if t == 0:
+            upstream[:, columns] = (
+                upstream[:, columns].astype(F32) + ADAPTER_SCALE * nn(low[...], down[:, columns])
+            ).astype(BF16)
+        dout = stacked(upstream, t, g)
+        out = stacked(attn, t, g)
+        delta = jnp.sum(dout.astype(F32) * out.astype(F32), axis=1, keepdims=True)
+        prob = probs[2 * g + t]
+        dscores = (prob * (nt(dout, values[t, :, head]) - delta)).astype(BF16)
+        dq = (nn(dscores, keys[t, :, head]) * scale).astype(BF16)
+        unstack(dquery, t, g, dq)
+        dk = tn(dscores, stacked(query, t, g)) * scale
+        dv = tn(prob.astype(BF16), dout)
+        back_send[t, :, head] = dk[0:half].astype(BF16)
+        back_send[t, :, tail] = dv[0:half].astype(BF16)
+        own_dkv[t, :, head] = dk[half:rows]
+        own_dkv[t, :, tail] = dv[half:rows]
+        if t == 1:
+            store = pltpu.make_async_copy(
+                dquery.at[:, columns], dquery_hbm.at[:, columns], store_sem.at[g]
+            )
+            store.start()
+            stores.append(store)
 
     backs = []
 
@@ -318,24 +339,17 @@
         def _():
             back_recv[0] = back_send[1]
 
-    for step in range(2 * levels):
-        if step < kv_heads:
-            backward(step)
-            if step == kv_heads - 1:
+    pieces = [(g, t) for g in range(kv_heads) for t in range(2)]
+    for step, which in events:
+        if pieces and which % 2 == 0:
+            backward(*pieces.pop(0))
+            if not pieces:
                 send_back()
-        for which in range(2):
-            end_step(which, step, flying[which])
-            if step + 1 < 2 * levels:
-                flying[which] = begin_step(which, step + 1)
-    for g in range(2 * levels, kv_heads):
-        backward(g)
-    if kv_heads > 2 * levels:
+        advance(step, which)
+    if pieces:
+        for piece in pieces:
+            backward(*piece)
         send_back()
-
-    for i in range(ctx_size):
-        columns = slice(i * slot_width, (i + 1) * slot_width)
-        ddown_ref[:, columns] = total[0, i].astype(F32)
-        dup_ref[:, columns] = total[1, i].astype(F32)
 
     @pl.when(jnp.logical_not(last))
     def _():
@@ -368,6 +382,32 @@
         halos[1].wait_send()
         halos[3].wait_send()
         backs[0].wait_send()
+
+
+def finish(
+    dquery_from, dkey_from, dvalue_from, total,
+    dquery_to, dkey_to, dvalue_to, ddown_to, dup_to, ddown, dup, sems,
+):
+    copies = [
+        pltpu.make_async_copy(src, dst, sems.at[i])
+        for i, (src, dst) in enumerate(
+            [(dquery_from, dquery_to), (dkey_from, dkey_to), (dvalue_from, dvalue_to)]
+        )
+    ]
+    for copy in copies:
+        copy.start()
+    cuts = total.shape[0] // 2
+    slots, _, slot_width = total.shape[1:]
+    for n, (block, result) in enumerate([(ddown, ddown_to), (dup, dup_to)]):
+        for c in range(cuts):
+            for i in range(slots):
+                start = (c * slots + i) * slot_width
+                block[:, start : start + slot_width] = total[n * cuts + c, i].astype(F32)
+        copy = pltpu.make_async_copy(block, result, sems.at[3 + n])
+        copy.start()
+        copies.append(copy)
+    for copy in copies:
+        copy.wait()
 
 
 def shards(
@@ -388,7 +428,10 @@
     half = rows // 2
     ctx_size = lax.axis_size("ctx")
     levels = ctx_size.bit_length() - 1
-    slot = (ctx_size, rank, width // ctx_size)
+    cuts = max(1, min(kv_heads, width // (ctx_size * 128)))
+    groups = (2 * cuts, ctx_size, rank, width // (ctx_size * cuts))
+    docs = document_length_list.shape[0]
+    inputs = pl.BlockSpec(memory_space=pltpu.HBM)
     anywhere = pl.BlockSpec(memory_space=pl.ANY)
     vmem = pl.BlockSpec(memory_space=pltpu.VMEM)
     dma = pltpu.SemaphoreType.DMA
@@ -398,11 +441,10 @@
             jax.ShapeDtypeStruct((rows, width), BF16),
             jax.ShapeDtypeStruct((rows, kv_width), BF16),
             jax.ShapeDtypeStruct((rows, kv_width), BF16),
-            jax.ShapeDtypeStruct((rank, width), F32),
-            jax.ShapeDtypeStruct((rank, model), F32),
+            jax.ShapeDtypeStruct(groups, BF16),
         ),
-        in_specs=[anywhere] * 7 + [vmem],
-        out_specs=(anywhere, vmem, vmem, vmem, vmem),
+        in_specs=[inputs] * 8,
+        out_specs=(anywhere, vmem, vmem, vmem),
         scratch_shapes=[
             pltpu.VMEM((rows, width), BF16),
             pltpu.VMEM((rows, width), BF16),
@@ -418,33 +460,49 @@
             pltpu.VMEM((rank, rows), F32),
             pltpu.VMEM((rank, rows), F32),
             pltpu.VMEM((rows, rank), BF16),
-            pltpu.VMEM((rank, rows), BF16),
             pltpu.VMEM((rank, rows), F32),
             pltpu.VMEM((rank, rows), F32),
             pltpu.VMEM((2, half, 2 * kv_width), F32),
             pltpu.VMEM((2, half, 2 * kv_width), BF16),
             pltpu.VMEM((2, half, 2 * kv_width), BF16),
-            pltpu.VMEM((2,) + slot, F32),
-            pltpu.VMEM((2,) + slot, BF16),
-            pltpu.VMEM((2,) + slot, BF16),
-            pltpu.VMEM((2,) + slot, BF16),
-            dma((9,)),
+            pltpu.VMEM(groups, F32),
+            pltpu.VMEM(groups, BF16),
+            pltpu.VMEM(groups, BF16),
+            pltpu.VMEM((1, docs), jnp.int32),
+            dma((10,)),
             dma((kv_heads,)),
             dma((2, 2)),
             dma((2, 2)),
             dma((4,)),
             dma((2, 2)),
-            dma((2, 2 * levels)),
-            dma((2, 2 * levels)),
+            dma((2 * cuts, 2 * levels)),
+            dma((2 * cuts, 2 * levels)),
         ],
         compiler_params=pltpu.CompilerParams(
-            collective_id=0, has_side_effects=True, vmem_limit_bytes=48 * 1024 * 1024
+            collective_id=0, has_side_effects=True, vmem_limit_bytes=63 * 1024 * 1024
         ),
     )(
         query, key_input, value, upstream, output_gradient, down_adapter.T, up_adapter,
         document_length_list[None, :],
     )
-    dquery, dkey, dvalue, ddown, dup = outs
+    results = (
+        jax.ShapeDtypeStruct((rows, width), BF16),
+        jax.ShapeDtypeStruct((rows, kv_width), BF16),
+        jax.ShapeDtypeStruct((rows, kv_width), BF16),
+        jax.ShapeDtypeStruct((rank, width), F32),
+        jax.ShapeDtypeStruct((rank, model), F32),
+    )
+    dquery, dkey, dvalue, ddown, dup = pl.pallas_call(
+        finish,
+        out_shape=results,
+        in_specs=[anywhere] * 3 + [vmem],
+        out_specs=(inputs,) * 5,
+        scratch_shapes=[
+            pltpu.VMEM((rank, width), F32),
+            pltpu.VMEM((rank, model), F32),
+            dma((5,)),
+        ],
+    )(*outs)
     return dquery, dkey, dvalue, ddown.T, dup
 
 

time: 64.5 us -> 128 us (1.98)
  Pallas kernels: 54.5 us -> 128 us
  local copies, waits for them, and re-layouts: 9.11 us -> 0 us
    pallas_call x0 -> x1, Pallas kernels: none -> 73.8 us  [shards(): pl.pallas_call(finish, out_shape=results, in_specs=[anywhere] * 3 + [vmem...]
    unnamed x15 -> x0, local copies, waits for them, and re-layouts: 9.11 us -> none
where the time goes in v2:
time: 128 us
  Pallas kernels  128 us (100%)
    pallas_call x1, Pallas kernels, shards(): pl.pallas_call(finish, out_shape=results, in_specs=[anywhere] * 3 + [vmem...  73.8 us
    pallas_call x1, Pallas kernels, shards(): pl.pallas_call(functools.partial(kernel, ctx_size), out_shape=(jax.ShapeD...  53.7 us

profile of v2, /device:TPU:0, one launch (start us, length us, event | category | flops | bytes accessed | tf_op | source)
XLA Modules:
  0.0 128.2 jit_solution(17549598050516258823)
XLA Ops:
  0.6 53.7 %shard_map.119 = (bf16[128,8192]{1,0:T(8,128)(2,1)}, bf16[128,512]{1,0:T(8,128)(2,1)}, bf16[128,512]{1,0:T(8,128)(2,1)}, bf16[8,8,32,256]{3,2,1,0:T(8,128)(2,1)}) custom-call(bf16[128,8192]{1,0:T(8,128)(2,1)} %query_hbm.1, bf16[128,512]{1,0:T(8,128)(2,1)} %key_hbm.1, bf16[128,512]{1,0:T(8,128)(2,1)} %value_hbm.1, bf16[128,8192]{1,0:T(8,128)(2,1)} %upstream_hbm.1, ...), custom_call_target="tpu_custom_call" | custom-call | tf_op jit(solution)/shard_map/pallas_call | solution.py:438
  54.3 73.8 %shard_map.120 = (bf16[128,8192]{1,0:T(8,128)(2,1)}, bf16[128,512]{1,0:T(8,128)(2,1)}, bf16[128,512]{1,0:T(8,128)(2,1)}, f32[32,8192]{1,0:T(8,128)}, f32[32,8192]{1,0:T(8,128)}) custom-call(bf16[128,8192]{1,0:T(8,128)(2,1)} %get-tuple-element.14.dquery_from, bf16[128,512]{1,0:T(8,128)(2,1)} %get-tuple-element.15.dkey_from, ...), custom_call_target="tpu_custom_call" | custom-call | tf_op jit(solution)/shard_map/pallas_call | solution.py:495

commit v3 on v2

--- a/solution.py
+++ b/solution.py
@@ -115,31 +115,31 @@
         barrier, 1 + levels + jnp.where(first, 0, 1) + jnp.where(last, 0, 1)
     )
 
-    def halo(hbm, buffer, which, t):
-        part = hbm.at[0:half] if t == 0 else hbm.at[half:rows]
-        target = me + 1 if t == 0 else me - 1
+    def halo(g, which, t):
+        hbm, buffer = ((key_hbm, keys), (value_hbm, values))[which]
+        head = slice(g * HEAD_SIZE, (g + 1) * HEAD_SIZE)
         return pltpu.make_async_remote_copy(
-            src_ref=part,
-            dst_ref=buffer.at[t, 0:half],
-            send_sem=halo_send_sem.at[which, t],
-            recv_sem=halo_recv_sem.at[which, t],
-            device_id={"ctx": target},
+            src_ref=hbm.at[t * half : (t + 1) * half, head],
+            dst_ref=buffer.at[t, 0:half, head],
+            send_sem=halo_send_sem.at[g, which, t],
+            recv_sem=halo_recv_sem.at[g, which, t],
+            device_id={"ctx": me + 1 if t == 0 else me - 1},
             device_id_type=MESH,
         )
 
-    halos = [halo(key_hbm, keys, 0, t) for t in range(2)] + [
-        halo(value_hbm, values, 1, t) for t in range(2)
-    ]
+    halos = [[[halo(g, which, t) for which in range(2)] for g in range(kv_heads)] for t in range(2)]
 
     @pl.when(jnp.logical_not(last))
     def _():
-        halos[0].start()
-        halos[2].start()
+        for pair in halos[0]:
+            for copy in pair:
+                copy.start()
 
     @pl.when(jnp.logical_not(first))
     def _():
-        halos[1].start()
-        halos[3].start()
+        for pair in halos[1]:
+            for copy in pair:
+                copy.start()
 
     loads[0].wait()
     loads[1].wait()
@@ -158,20 +158,21 @@
         keys[0, 0:half] = jnp.zeros((half, kv_width), BF16)
         values[0, 0:half] = jnp.zeros((half, kv_width), BF16)
 
-    @pl.when(jnp.logical_not(first))
-    def _():
-        halos[0].wait_recv()
-        halos[2].wait_recv()
-
     @pl.when(last)
     def _():
         keys[1, 0:half] = keys[0, half:rows]
         values[1, 0:half] = values[0, half:rows]
 
-    @pl.when(jnp.logical_not(last))
-    def _():
-        halos[1].wait_recv()
-        halos[3].wait_recv()
+    def halo_wait(g):
+        @pl.when(jnp.logical_not(first))
+        def _():
+            for copy in halos[0][g]:
+                copy.wait_recv()
+
+        @pl.when(jnp.logical_not(last))
+        def _():
+            for copy in halos[1][g]:
+                copy.wait_recv()
 
     def stacked(ref, t, g):
         return jnp.concatenate(
@@ -186,10 +187,6 @@
         for h in range(group):
             start = g * group_width + h * HEAD_SIZE
             ref[t * half : (t + 1) * half, start : start + HEAD_SIZE] = block[h * half : (h + 1) * half]
-
-    low_copy.wait_recv()
-    low_t = (low_send[...] + low_recv[...]).astype(BF16)
-    low[...] = (low_send[...] + low_recv[...]).T.astype(BF16)
 
     slot_width = acc.shape[3]
     started = []
@@ -254,6 +251,7 @@
     outer = jnp.zeros((rows, low_send.shape[0]), F32)
     for g in range(kv_heads):
         head = slice(g * HEAD_SIZE, (g + 1) * HEAD_SIZE)
+        halo_wait(g)
         for t in range(2):
             scores = nt(stacked(query, t, g), keys[t, :, head]) * scale
             scores = scores.reshape(group, half, rows) + bias[t][None]
@@ -272,6 +270,10 @@
                 device_id={"tp": 1 - tp}, device_id_type=MESH,
             )
             outer_copy.start()
+        if g == 0:
+            low_copy.wait_recv()
+            low_t = (low_send[...] + low_recv[...]).astype(BF16)
+            low[...] = (low_send[...] + low_recv[...]).T.astype(BF16)
         for which in range(cuts):
             if (which + 1) * kv_heads // cuts == g + 1:
                 fill(which, low_t, attn)
@@ -341,7 +343,7 @@
 
     pieces = [(g, t) for g in range(kv_heads) for t in range(2)]
     for step, which in events:
-        if pieces and which % 2 == 0:
+        if pieces and (which % 2 == 0 or step > 1):
             backward(*pieces.pop(0))
             if not pieces:
                 send_back()
@@ -373,29 +375,38 @@
 
     @pl.when(jnp.logical_not(last))
     def _():
-        halos[0].wait_send()
-        halos[2].wait_send()
+        for pair in halos[0]:
+            for copy in pair:
+                copy.wait_send()
         backs[1].wait_send()
 
     @pl.when(jnp.logical_not(first))
     def _():
-        halos[1].wait_send()
-        halos[3].wait_send()
+        for pair in halos[1]:
+            for copy in pair:
+                copy.wait_send()
         backs[0].wait_send()
 
 
 def finish(
-    dquery_from, dkey_from, dvalue_from, total,
-    dquery_to, dkey_to, dvalue_to, ddown_to, dup_to, ddown, dup, sems,
+    dquery_from, dkey_from, dvalue_from, total_from,
+    dquery_to, dkey_to, dvalue_to, ddown_to, dup_to,
+    dquery, dkey, dvalue, total, ddown, dup, in_sems, out_sems,
 ):
-    copies = [
-        pltpu.make_async_copy(src, dst, sems.at[i])
-        for i, (src, dst) in enumerate(
-            [(dquery_from, dquery_to), (dkey_from, dkey_to), (dvalue_from, dvalue_to)]
-        )
+    strip = dquery.shape[0] // 4
+    moves = [
+        (total_from, total, None),
+        (dkey_from, dkey, dkey_to),
+        (dvalue_from, dvalue, dvalue_to),
+    ] + [
+        (dquery_from.at[part], dquery.at[part], dquery_to.at[part])
+        for part in [pl.ds(i * strip, strip) for i in range(4)]
     ]
-    for copy in copies:
+    ins = [pltpu.make_async_copy(m[0], m[1], in_sems.at[i]) for i, m in enumerate(moves)]
+    for copy in ins:
         copy.start()
+    outs = []
+    ins[0].wait()
     cuts = total.shape[0] // 2
     slots, _, slot_width = total.shape[1:]
     for n, (block, result) in enumerate([(ddown, ddown_to), (dup, dup_to)]):
@@ -403,10 +414,13 @@
             for i in range(slots):
                 start = (c * slots + i) * slot_width
                 block[:, start : start + slot_width] = total[n * cuts + c, i].astype(F32)
-        copy = pltpu.make_async_copy(block, result, sems.at[3 + n])
-        copy.start()
-        copies.append(copy)
-    for copy in copies:
+        outs.append(pltpu.make_async_copy(block, result, out_sems.at[n]))
+        outs[-1].start()
+    for i in range(1, len(moves)):
+        ins[i].wait()
+        outs.append(pltpu.make_async_copy(moves[i][1], moves[i][2], out_sems.at[i + 1]))
+        outs[-1].start()
+    for copy in outs:
         copy.wait()
 
 
@@ -471,8 +485,8 @@
             pltpu.VMEM((1, docs), jnp.int32),
             dma((10,)),
             dma((kv_heads,)),
-            dma((2, 2)),
-            dma((2, 2)),
+            dma((kv_heads, 2, 2)),
+            dma((kv_heads, 2, 2)),
             dma((4,)),
             dma((2, 2)),
             dma((2 * cuts, 2 * levels)),
@@ -495,13 +509,19 @@
     dquery, dkey, dvalue, ddown, dup = pl.pallas_call(
         finish,
         out_shape=results,
-        in_specs=[anywhere] * 3 + [vmem],
+        in_specs=[anywhere] * 4,
         out_specs=(inputs,) * 5,
         scratch_shapes=[
+            pltpu.VMEM((rows, width), BF16),
+            pltpu.VMEM((rows, kv_width), BF16),
+            pltpu.VMEM((rows, kv_width), BF16),
+            pltpu.VMEM(groups, BF16),
             pltpu.VMEM((rank, width), F32),
             pltpu.VMEM((rank, model), F32),
-            dma((5,)),
+            dma((7,)),
+            dma((8,)),
         ],
+        compiler_params=pltpu.CompilerParams(vmem_limit_bytes=63 * 1024 * 1024),
     )(*outs)
     return dquery, dkey, dvalue, ddown.T, dup
 

time: 128 us -> 56.6 us (0.44)
  Pallas kernels: 128 us -> 55.8 us
    pallas_call x1, Pallas kernels: 73.8 us -> 3.51 us  [shards(): pl.pallas_call(finish, out_shape=results, in_specs=[anywhere] * 4, out_sp...]
    pallas_call x1, Pallas kernels: 53.7 us -> 52.3 us  [shards(): pl.pallas_call(functools.partial(kernel, ctx_size), out_shape=(jax.ShapeD...]
where the time goes in v3:
time: 56.6 us; the launch traced here: 56.5 us
  Pallas kernels  55.8 us (99%)
  between operations  0.64 us (1%)
    pallas_call x1, Pallas kernels, shards(): pl.pallas_call(functools.partial(kernel, ctx_size), out_shape=(jax.ShapeD...  52.3 us
    pallas_call x1, Pallas kernels, shards(): pl.pallas_call(finish, out_shape=results, in_specs=[anywhere] * 4, out_sp...  3.51 us

profile of v3, /device:TPU:0, one launch (start us, length us, event | category | flops | bytes accessed | tf_op | source)
XLA Modules:
  0.0 56.5 jit_solution(11085077046844978208)
XLA Ops:
  0.6 52.3 %shard_map.119 = (bf16[128,8192]{1,0:T(8,128)(2,1)}, bf16[128,512]{1,0:T(8,128)(2,1)}, bf16[128,512]{1,0:T(8,128)(2,1)}, bf16[8,8,32,256]{3,2,1,0:T(8,128)(2,1)}) custom-call(bf16[128,8192]{1,0:T(8,128)(2,1)} %query_hbm.1, bf16[128,512]{1,0:T(8,128)(2,1)} %key_hbm.1, bf16[128,512]{1,0:T(8,128)(2,1)} %value_hbm.1, bf16[128,8192]{1,0:T(8,128)(2,1)} %upstream_hbm.1, ...), custom_call_target="tpu_custom_call" | custom-call | tf_op jit(solution)/shard_map/pallas_call | solution.py:452
  53.0 3.5 %shard_map.120 = (bf16[128,8192]{1,0:T(8,128)(2,1)}, bf16[128,512]{1,0:T(8,128)(2,1)}, bf16[128,512]{1,0:T(8,128)(2,1)}, f32[32,8192]{1,0:T(8,128)}, f32[32,8192]{1,0:T(8,128)}) custom-call(bf16[128,8192]{1,0:T(8,128)(2,1)} %get-tuple-element.14.dquery_from, bf16[128,512]{1,0:T(8,128)(2,1)} %get-tuple-element.15.dkey_from, ...), custom_call_target="tpu_custom_call" | custom-call | tf_op jit(solution)/shard_map/pallas_call | solution.py:509

commit v4 on v3

--- a/solution.py
+++ b/solution.py
@@ -58,7 +58,7 @@
     for i in range(0, levels - 1, 2):
         swapped[i], swapped[i + 1] = i + 1, i
     orders = [
-        swapped if w < cuts and w % 2 == 0 or w == cuts + 1 else list(range(levels))
+        swapped if w % 2 == 0 else list(range(levels))
         for w in range(2 * cuts)
     ]
 
@@ -277,12 +277,6 @@
         for which in range(cuts):
             if (which + 1) * kv_heads // cuts == g + 1:
                 fill(which, low_t, attn)
-    outer_copy.wait_recv()
-    outer_sum = (outer_send[...] + outer_recv[...]).astype(BF16)
-    for which in range(cuts):
-        fill(cuts + which, outer_sum, grad)
-    loads[8].wait()
-
     stores = []
 
     def backward(g, t):
@@ -313,6 +307,13 @@
             store.start()
             stores.append(store)
 
+    pieces = [(g, t) for g in range(kv_heads) for t in range(2)]
+    loads[8].wait()
+    backward(*pieces.pop(0))
+    outer_copy.wait_recv()
+    outer_sum = (outer_send[...] + outer_recv[...]).astype(BF16)
+    for which in range(cuts):
+        fill(cuts + which, outer_sum, grad)
     backs = []
 
     def send_back():
@@ -341,7 +342,6 @@
         def _():
             back_recv[0] = back_send[1]
 
-    pieces = [(g, t) for g in range(kv_heads) for t in range(2)]
     for step, which in events:
         if pieces and (which % 2 == 0 or step > 1):
             backward(*pieces.pop(0))

time: 56.6 us -> 55.2 us (0.975)
  Pallas kernels: 55.8 us -> 54.4 us
    pallas_call x1, Pallas kernels: 52.3 us -> 50.9 us  [shards(): pl.pallas_call(functools.partial(kernel, ctx_size), out_shape=(jax.ShapeD...]
where the time goes in v4:
time: 55.2 us; the launch traced here: 55.1 us
  Pallas kernels  54.4 us (99%)
  between operations  0.64 us (1%)
    pallas_call x1, Pallas kernels, shards(): pl.pallas_call(functools.partial(kernel, ctx_size), out_shape=(jax.ShapeD...  50.9 us
    pallas_call x1, Pallas kernels, shards(): pl.pallas_call(finish, out_shape=results, in_specs=[anywhere] * 4, out_sp...  3.51 us

profile of v4, /device:TPU:0, one launch (start us, length us, event | category | flops | bytes accessed | tf_op | source)
XLA Modules:
  0.0 55.1 jit_solution(5030495129251995817)
XLA Ops:
  0.6 50.9 %shard_map.119 = (bf16[128,8192]{1,0:T(8,128)(2,1)}, bf16[128,512]{1,0:T(8,128)(2,1)}, bf16[128,512]{1,0:T(8,128)(2,1)}, bf16[8,8,32,256]{3,2,1,0:T(8,128)(2,1)}) custom-call(bf16[128,8192]{1,0:T(8,128)(2,1)} %query_hbm.1, bf16[128,512]{1,0:T(8,128)(2,1)} %key_hbm.1, bf16[128,512]{1,0:T(8,128)(2,1)} %value_hbm.1, bf16[128,8192]{1,0:T(8,128)(2,1)} %upstream_hbm.1, ...), custom_call_target="tpu_custom_call" | custom-call | tf_op jit(solution)/shard_map/pallas_call | solution.py:452
  51.6 3.5 %shard_map.120 = (bf16[128,8192]{1,0:T(8,128)(2,1)}, bf16[128,512]{1,0:T(8,128)(2,1)}, bf16[128,512]{1,0:T(8,128)(2,1)}, f32[32,8192]{1,0:T(8,128)}, f32[32,8192]{1,0:T(8,128)}) custom-call(bf16[128,8192]{1,0:T(8,128)(2,1)} %get-tuple-element.14.dquery_from, bf16[128,512]{1,0:T(8,128)(2,1)} %get-tuple-element.15.dkey_from, ...), custom_call_target="tpu_custom_call" | custom-call | tf_op jit(solution)/shard_map/pallas_call | solution.py:509
